TPU v7x, 32 devices: a whole 2x2x4 slice. The times are simulated.
32 devices in a mesh: blk: 16 (over z, y, x), layer: 2 (over core).
Axes of the slice: x: 2, y: 2, z: 4, core: 2. Of those that a mesh axis runs over, the one named last changes fastest.
Arguments:
- train_factors: bfloat16 [192, 2, 2, 64, 1024], P('blk', 'layer'), may hold values from -0.29882812 to 0.29882812
- val_factors: bfloat16 [64, 2, 2, 64, 1024], P('blk', 'layer'), may hold values from -0.29882812 to 0.29882812
Outputs:
- scores: float32 [192, 3, 4], P('blk')
All inputs are finite; a program needn't handle non-finite values.
Results may differ from a plain program's by a relative error of at most 0.0003.
Values may be sent and summed in bfloat16 or wider, within the bound.
No kernel may reach another device: no remote copies, remote signals or barrier semaphores. Data moves between devices by JAX's collectives and lax.ppermute only.
A program may use at most 64 MiB of HBM per device.

v0:
```python
import functools

import jax
import jax.numpy as jnp
from jax import lax
from jax.experimental import pallas as pl
from jax.experimental.pallas import tpu as pltpu
from jax.sharding import PartitionSpec as P

CUTS = 4
GROUP = 4

VMEM = pl.BlockSpec(memory_space=pltpu.VMEM)


def permuted(block, axis, target):
    size = lax.axis_size(axis)
    return lax.ppermute(block, axis, [(i, target(i) % size) for i in range(size)])


def call(kernel, out_shape, specs, operands, flops=0, scratch=(), vmem=16 << 20):
    shapes = list(operands) + jax.tree.leaves(out_shape)
    return pl.pallas_call(
        kernel,
        out_shape=out_shape,
        in_specs=specs,
        out_specs=jax.tree.map(lambda _: VMEM, out_shape),
        scratch_shapes=scratch,
        compiler_params=pltpu.CompilerParams(vmem_limit_bytes=vmem),
        cost_estimate=pl.CostEstimate(
            flops=flops,
            bytes_accessed=sum(x.size * x.dtype.itemsize for x in shapes),
            transcendentals=0,
        ),
    )(*operands)


def groups(train_ref):
    examples = train_ref.shape[0]
    size = GROUP if examples % GROUP == 0 else 1
    return [slice(first, first + size) for first in range(0, examples, size)]


def gram(train_ref, val_refs, layer, index, group, start=0):
    total = 0.0
    for ref in val_refs:
        depth = ref.shape[-1]
        train = train_ref[group, layer, index, :, start : start + depth].reshape(-1, depth)
        val = ref[:, layer, index].reshape(-1, depth)
        total = total + lax.dot_general(
            train, val, (((1,), (1,)), ((), ())), preferred_element_type=jnp.float32
        )
        start += depth
    return total


def token_sums(product, tokens):
    return jnp.sum(product.reshape(-1, tokens, product.shape[-1]), axis=1)


def example_sums(by_token, tokens):
    count = by_token.shape[-1] // tokens
    shape = (count, by_token.shape[-1])
    token = lax.broadcasted_iota(jnp.int32, shape, 1) // tokens
    mine = (token == lax.broadcasted_iota(jnp.int32, shape, 0)).astype(jnp.bfloat16)
    total, rest = 0.0, by_token
    for _ in range(3):
        piece = rest.astype(jnp.bfloat16)
        rest = rest - piece.astype(jnp.float32)
        total = total + lax.dot_general(
            mine, piece, (((1,), (1,)), ((), ())), preferred_element_type=jnp.float32
        )
    return total


def scores(train_ref, val_refs):
    layers, tokens = train_ref.shape[1], train_ref.shape[3]
    sums = []
    for group in groups(train_ref):
        product = 0.0
        for layer in range(layers):
            product = product + gram(train_ref, val_refs, layer, 0, group) * gram(
                train_ref, val_refs, layer, 1, group
            )
        sums.append(token_sums(product, tokens))
    return example_sums(jnp.concatenate(sums, axis=0), tokens)


def cut_kernel(val_ref, *refs):
    *part_refs, joint_ref = refs
    for c, ref in enumerate(part_refs, 1):
        depth = ref.shape[-1]
        ref[...] = val_ref[..., c * depth : (c + 1) * depth]
    count = val_ref.shape[0]
    joint_ref[:count] = part_refs[-2][...]
    joint_ref[count:] = part_refs[-1][count - 1 :]


def scores_kernel(train_ref, *refs):
    *val_refs, out_ref = refs
    out_ref[...] = scores(train_ref, val_refs)


def by_parity(even, odd):
    parity = lax.rem(lax.axis_index("blk"), 2)
    pl.when(parity == 0)(even)
    pl.when(parity == 1)(odd)


def pick_kernel(even_ref, odd_ref, *refs):
    out_ref = refs[-1]

    def put(ref):
        out_ref[...] = ref[...]

    by_parity(lambda: put(even_ref), lambda: put(odd_ref))


def columns(first, count, tokens):
    return slice(first * tokens, (first + count) * tokens)


def grams_kernel(train_ref, *refs):
    *part_refs, out_ref = refs
    layers, tokens = train_ref.shape[1], train_ref.shape[3]
    for layer in range(layers):
        for index in range(2):
            for group in groups(train_ref):
                rows = slice(group.start * tokens, group.stop * tokens)
                out_ref[layer, index, rows] = gram(train_ref, part_refs, layer, index, group)


def far_kernel(train_ref, *refs):
    *part_refs, joint_ref, out_ref = refs
    grams_kernel(train_ref, *part_refs, joint_ref.at[: part_refs[0].shape[0]], out_ref)


def second_kernel(train_ref, detour_ref, joint_ref, grams_ref, out_ref):
    layers, tokens, features = train_ref.shape[1], train_ref.shape[3], train_ref.shape[4]
    start, split, count = features - detour_ref.shape[-1], detour_ref.shape[0], out_ref.shape[0]
    for first, stop, ref in ((0, split, detour_ref), (split, count, joint_ref.at[count:])):
        cols = columns(first, stop - first, tokens)
        sums = []
        for group in groups(train_ref):
            rows = slice(group.start * tokens, group.stop * tokens)
            product = 0.0
            for layer in range(layers):
                act, grad = (
                    grams_ref[layer, index, rows, cols] + gram(train_ref, [ref], layer, index, group, start)
                    for index in range(2)
                )
                product = product + act * grad
            sums.append(token_sums(product, tokens))
        out_ref[first:stop] = example_sums(jnp.concatenate(sums, axis=0), tokens)


def add_kernel(train_ref, far_ref, near_ref, grams_ref, out_ref):
    layers, tokens, features = train_ref.shape[1], train_ref.shape[3], train_ref.shape[4]
    detour = columns(0, far_ref.shape[0], tokens)
    rest = slice(detour.stop, grams_ref.shape[-1])

    def add(last_ref):
        begin = features - last_ref.shape[-1]
        for layer in range(layers):
            for index in range(2):
                for group in groups(train_ref):
                    rows = slice(group.start * tokens, group.stop * tokens)
                    out_ref[layer, index, rows, detour] = grams_ref[layer, index, rows, detour] + gram(
                        train_ref, [last_ref], layer, index, group, begin
                    )

    out_ref[..., rest] = grams_ref[..., rest]
    by_parity(lambda: add(far_ref), lambda: add(near_ref))


def last_kernel(train_ref, joint_ref, grams_ref, own_ref, second_ref, out_ref):
    layers, tokens, features = train_ref.shape[1], train_ref.shape[3], train_ref.shape[4]
    depth, count = joint_ref.shape[-1], out_ref.shape[1]
    split = 2 * count - joint_ref.shape[0]
    cols = (columns(0, split, tokens), columns(split, count - split, tokens))
    sums = ([], [])
    for group in groups(train_ref):
        rows = slice(group.start * tokens, group.stop * tokens)
        products = [0.0, 0.0]
        for layer in range(layers):
            totals = [
                grams_ref[layer, index, rows]
                + gram(train_ref, [joint_ref.at[:count]], layer, index, group, features - 2 * depth)
                for index in range(2)
            ]
            for n in range(2):
                act, grad = (total[:, cols[n]] for total in totals)
                if n == 1:
                    ends = [
                        gram(train_ref, [joint_ref.at[count:]], layer, index, group, features - depth)
                        for index in range(2)
                    ]
                    act, grad = act + ends[0], grad + ends[1]
                products[n] = products[n] + act * grad
        for n in range(2):
            sums[n].append(token_sums(products[n], tokens))
    out_ref[0] = own_ref[...]
    out_ref[1, :split] = example_sums(jnp.concatenate(sums[0], axis=0), tokens)
    out_ref[1, split:] = example_sums(jnp.concatenate(sums[1], axis=0), tokens)
    out_ref[2] = second_ref[...]


def summed(rows, axis):
    if lax.axis_size(axis) != 2:
        return lax.psum(rows, axis)
    return rows + permuted(rows, axis, lambda i: i ^ 1)


def local(train, val):
    examples, layers, _, tokens, features = train.shape
    count = val.shape[0]
    cuts = CUTS
    depth = features // cuts
    work = 4 * examples * count * layers * tokens * tokens * features
    part = jax.ShapeDtypeStruct(val.shape[:-1] + (depth,), val.dtype)
    rows = jax.ShapeDtypeStruct((count, examples), jnp.float32)
    grams = jax.ShapeDtypeStruct((layers, 2, examples * tokens, count * tokens), jnp.float32)

    detour = val[: count - 1, ..., (cuts - 1) * depth :]
    joint = jax.ShapeDtypeStruct((count + 1,) + part.shape[1:], val.dtype)
    *parts, joint = call(cut_kernel, [part] * (cuts - 1) + [joint], [VMEM], [val])
    parts = [val[..., :depth]] + parts
    second = [permuted(x, "blk", lambda i: i + 2) for x in parts[:-2] + [joint]]
    near_last = permuted(detour, "blk", lambda i: i ^ 1)
    second_detour = permuted(detour, "blk", lambda i: i + 2)
    far_last = permuted(near_last, "blk", lambda i: i + 2)
    first = []
    for c in range(cuts - 2):
        operands = [parts[c], second[c]] + ([near_last] if c == 1 else [])
        picked = call(pick_kernel, part, [VMEM] * len(operands), operands)
        first.append(permuted(picked, "blk", lambda i: i ^ 1))
    shape = jax.ShapeDtypeStruct(joint.shape, joint.dtype)
    picked = call(pick_kernel, shape, [VMEM] * 2, [joint, second[-1]])
    first.append(permuted(picked, "blk", lambda i: i ^ 1))
    sums = call(grams_kernel, grams, [VMEM] * (cuts - 1), [train] + first[:-1], work // 2)
    far = call(far_kernel, grams, [VMEM] * cuts, [train] + second, work)

    own = call(scores_kernel, rows, [VMEM] * (1 + cuts), [train] + parts, work)
    operands = [train, second_detour, second[-1], far]
    far = call(second_kernel, rows, [VMEM] * len(operands), operands, work // 4)
    sums = call(add_kernel, grams, [VMEM] * 4, [train, far_last, near_last, sums], 2 * work)
    out = jax.ShapeDtypeStruct((3,) + rows.shape, jnp.float32)
    operands = [train, first[-1], sums, own, far]
    partial_rows = call(last_kernel, out, [VMEM] * len(operands), operands, work // 4)
    return summed(partial_rows, "layer").transpose(2, 0, 1)


def solution(mesh):
    return jax.shard_map(
        local,
        mesh=mesh,
        in_specs=(P("blk", "layer", None, None, None), P("blk", "layer", None, None, None)),
        out_specs=P("blk", None, None),
        check_vma=False,
    )
```

profile of v0, /device:TPU:0, one launch (start us, length us, event | category | flops | bytes accessed | tf_op | source)
XLA Modules:
  0.0 37.6 jit_solution(14003521105152315334)
XLA Ops:
  0.0 1.0 %slice.7.even_ref.refs_0_ = bf16[4,1,2,64,256]{4,3,2,1,0:T(8,128)(2,1)S(1)} slice(bf16[4,1,2,64,1024]{4,3,2,1,0:T(8,128)(2,1)} %val_ref.1), slice={[0:4], [0:1], [0:2], [0:64], [0:256]} | slice | bytes 524288 | tf_op jit(solution)/shard_map/slice | solution.py:227
  1.0 3.0 %collective-permute-start.4 = (bf16[4,1,2,64,256]{4,3,2,1,0:T(8,128)(2,1)S(1)}, bf16[4,1,2,64,256]{4,3,2,1,0:T(8,128)(2,1)S(1)}, u32[]{:S(2)}, u32[]{:S(2)}) collective-permute-start(bf16[4,1,2,64,256]{4,3,2,1,0:T(8,128)(2,1)S(1)} %slice.7.even_ref.refs_0_), channel_id=1, source_target_pairs={{0,4},{2,6},{4,8},{6,10},{8,12},{10,14},{12,16},{14,18},{16,20},{1... | collective-permute-start | bytes 786440 | tf_op jit(solution)/shard_map/ppermute | solution.py:18
  4.0 0.0 copy-start.1
  4.0 1.2 %copy-done.1 = bf16[4,1,2,64,1024]{4,3,2,1,0:T(8,128)(2,1)S(1)} copy-done((bf16[4,1,2,64,1024]{4,3,2,1,0:T(8,128)(2,1)S(1)}, bf16[4,1,2,64,1024]{4,3,2,1,0:T(8,128)(2,1)}, u32[]{:S(2)}) %copy-start.1) | copy-done | bytes 1048600
  5.2 0.1 shard_map.28
  5.3 1.6 %collective-permute-start.6 = (bf16[4,1,2,64,256]{4,3,2,1,0:T(8,128)(2,1)S(1)}, bf16[4,1,2,64,256]{4,3,2,1,0:T(8,128)(2,1)S(1)}, u32[]{:S(2)}, u32[]{:S(2)}) collective-permute-start(bf16[4,1,2,64,256]{4,3,2,1,0:T(8,128)(2,1)S(1)} %get-tuple-element.10.even_ref.refs_1_), channel_id=1, source_target_pairs={{0,4},{2,6},{4,8},{6,10},{8,12},{10,14},{12,16},{14,18},{16,20},{1... | collective-permute-start | bytes 786440 | tf_op jit(solution)/shard_map/ppermute | solution.py:18
  6.9 0.0 copy-start
  6.9 1.5 %collective-permute-start = (bf16[5,1,2,64,256]{4,3,2,1,0:T(8,128)(2,1)S(1)}, bf16[5,1,2,64,256]{4,3,2,1,0:T(8,128)(2,1)S(1)}, u32[]{:S(2)}, u32[]{:S(2)}) collective-permute-start(bf16[5,1,2,64,256]{4,3,2,1,0:T(8,128)(2,1)S(1)} %get-tuple-element.9.even_ref), channel_id=1, source_target_pairs={{0,4},{2,6},{4,8},{6,10},{8,12},{10,14},{12,16},{14,18},{16,20},{1... | collective-permute-start | bytes 983048 | tf_op jit(solution)/shard_map/ppermute | solution.py:18
  8.4 1.6 %collective-permute-start.2 = (bf16[3,1,2,64,256]{4,3,2,1,0:T(8,128)(2,1)S(1)}, bf16[3,1,2,64,256]{4,3,2,1,0:T(8,128)(2,1)S(1)}, u32[]{:S(2)}, u32[]{:S(2)}) collective-permute-start(bf16[3,1,2,64,256]{4,3,2,1,0:T(8,128)(2,1)S(1)} %slice.6), channel_id=1, source_target_pairs={{0,2},{2,0},{4,6},{6,4},{8,10},{10,8},{12,14},{14,12},{16,18},{18,... | collective-permute-start | bytes 589832 | tf_op jit(solution)/shard_map/ppermute | solution.py:18
  10.0 4.2 %collective-permute-done.4.odd_ref.refs_0_ = bf16[4,1,2,64,256]{4,3,2,1,0:T(8,128)(2,1)S(1)} collective-permute-done((bf16[4,1,2,64,256]{4,3,2,1,0:T(8,128)(2,1)S(1)}, bf16[4,1,2,64,256]{4,3,2,1,0:T(8,128)(2,1)S(1)}, u32[]{:S(2)}, u32[]{:S(2)}) %collective-permute-start.4) | collective-permute-done | bytes 262176 | tf_op jit(solution)/shard_map/ppermute | solution.py:18
  14.2 1.7 %collective-permute-start.5 = (bf16[4,1,2,64,256]{4,3,2,1,0:T(8,128)(2,1)S(1)}, bf16[4,1,2,64,256]{4,3,2,1,0:T(8,128)(2,1)S(1)}, u32[]{:S(2)}, u32[]{:S(2)}) collective-permute-start(bf16[4,1,2,64,256]{4,3,2,1,0:T(8,128)(2,1)S(1)} %shard_map.30), channel_id=1, source_target_pairs={{0,2},{2,0},{4,6},{6,4},{8,10},{10,8},{12,14},{14,12},{16,18},{18,... | collective-permute-start | bytes 786440 | tf_op jit(solution)/shard_map/ppermute | solution.py:18
  15.9 0.0 collective-permute-done.2.refs_0_.near_ref
  15.9 3.9 %collective-permute-done.6.odd_ref.refs_1_ = bf16[4,1,2,64,256]{4,3,2,1,0:T(8,128)(2,1)S(1)} collective-permute-done((bf16[4,1,2,64,256]{4,3,2,1,0:T(8,128)(2,1)S(1)}, bf16[4,1,2,64,256]{4,3,2,1,0:T(8,128)(2,1)S(1)}, u32[]{:S(2)}, u32[]{:S(2)}) %collective-permute-start.6) | collective-permute-done | bytes 262176 | tf_op jit(solution)/shard_map/ppermute | solution.py:18
  19.8 1.7 %collective-permute-start.7 = (bf16[4,1,2,64,256]{4,3,2,1,0:T(8,128)(2,1)S(1)}, bf16[4,1,2,64,256]{4,3,2,1,0:T(8,128)(2,1)S(1)}, u32[]{:S(2)}, u32[]{:S(2)}) collective-permute-start(bf16[4,1,2,64,256]{4,3,2,1,0:T(8,128)(2,1)S(1)} %shard_map.31), channel_id=1, source_target_pairs={{0,2},{2,0},{4,6},{6,4},{8,10},{10,8},{12,14},{14,12},{16,18},{18,... | collective-permute-start | bytes 786440 | tf_op jit(solution)/shard_map/ppermute | solution.py:18
  21.5 0.0 collective-permute-start.8
  21.5 1.3 %collective-permute-start.3 = (bf16[3,1,2,64,256]{4,3,2,1,0:T(8,128)(2,1)S(1)}, bf16[3,1,2,64,256]{4,3,2,1,0:T(8,128)(2,1)S(1)}, u32[]{:S(2)}, u32[]{:S(2)}) collective-permute-start(bf16[3,1,2,64,256]{4,3,2,1,0:T(8,128)(2,1)S(1)} %collective-permute-done.2.refs_0_.near_ref), channel_id=1, source_target_pairs={{0,4},{2,6},{4,8},{6,10},{8,12},{10,14},{12,16},{14,18},{16,20},{1... | collective-permute-start | bytes 589832 | tf_op jit(solution)/shard_map/ppermute | solution.py:18
  22.8 4.0 %collective-permute-done.odd_ref.refs_2_.joint_ref = bf16[5,1,2,64,256]{4,3,2,1,0:T(8,128)(2,1)S(1)} collective-permute-done((bf16[5,1,2,64,256]{4,3,2,1,0:T(8,128)(2,1)S(1)}, bf16[5,1,2,64,256]{4,3,2,1,0:T(8,128)(2,1)S(1)}, u32[]{:S(2)}, u32[]{:S(2)}) %collective-permute-start) | collective-permute-done | bytes 327712 | tf_op jit(solution)/shard_map/ppermute | solution.py:18
  26.8 1.7 %collective-permute-start.1 = (bf16[5,1,2,64,256]{4,3,2,1,0:T(8,128)(2,1)S(1)}, bf16[5,1,2,64,256]{4,3,2,1,0:T(8,128)(2,1)S(1)}, u32[]{:S(2)}, u32[]{:S(2)}) collective-permute-start(bf16[5,1,2,64,256]{4,3,2,1,0:T(8,128)(2,1)S(1)} %shard_map.29), channel_id=1, source_target_pairs={{0,2},{2,0},{4,6},{6,4},{8,10},{10,8},{12,14},{14,12},{16,18},{18,... | collective-permute-start | bytes 983048 | tf_op jit(solution)/shard_map/ppermute | solution.py:18
  28.6 0.0 copy-done
  28.6 1.1 %shard_map.34.own_ref = f32[4,12]{1,0:T(4,128)S(1)} custom-call(bf16[12,1,2,64,1024]{4,3,2,1,0:T(8,128)(2,1)S(1)} %copy-done, bf16[4,1,2,64,256]{4,3,2,1,0:T(8,128)(2,1)S(1)} %slice.7.even_ref.refs_0_, bf16[4,1,2,64,256]{4,3,2,1,0:T(8,128)(2,1)S(1)} %get-tuple-element.10.even_ref.refs_1_, bf16[4,1,2,64,256]{4,3,2,1,0:T(8,128)(2,1)S(1)} %get-tuple-element.11.refs_2_, ...), custom_call_target="tpu_custom_call" | custom-call | flops 805306368 | bytes 4194496 | tf_op jit(solution)/shard_map/pallas_call | solution.py:23
  29.7 0.8 %shard_map.35.grams_ref = f32[1,2,768,256]{3,2,1,0:T(8,128)S(1)} custom-call(bf16[12,1,2,64,1024]{4,3,2,1,0:T(8,128)(2,1)S(1)} %copy-done, bf16[4,1,2,64,256]{4,3,2,1,0:T(8,128)(2,1)S(1)} %collective-permute-done.4.odd_ref.refs_0_, bf16[4,1,2,64,256]{4,3,2,1,0:T(8,128)(2,1)S(1)} %collective-permute-done.6.odd_ref.refs_1_, ...), custom_call_target="tpu_custom_call" | custom-call | flops 805306368 | bytes 5570560 | tf_op jit(solution)/shard_map/pallas_call | solution.py:23
  30.6 1.5 %collective-permute-done.8.detour_ref = bf16[3,1,2,64,256]{4,3,2,1,0:T(8,128)(2,1)S(1)} collective-permute-done((bf16[3,1,2,64,256]{4,3,2,1,0:T(8,128)(2,1)S(1)}, bf16[3,1,2,64,256]{4,3,2,1,0:T(8,128)(2,1)S(1)}, u32[]{:S(2)}, u32[]{:S(2)}) %collective-permute-start.8) | collective-permute-done | bytes 196640 | tf_op jit(solution)/shard_map/ppermute | solution.py:18
  32.1 1.0 %shard_map.36.second_ref = f32[4,12]{1,0:T(4,128)S(1)} custom-call(bf16[12,1,2,64,1024]{4,3,2,1,0:T(8,128)(2,1)S(1)} %copy-done, bf16[3,1,2,64,256]{4,3,2,1,0:T(8,128)(2,1)S(1)} %collective-permute-done.8.detour_ref, bf16[5,1,2,64,256]{4,3,2,1,0:T(8,128)(2,1)S(1)} %collective-permute-done.odd_ref.refs_2_.joint_ref, f32[1,2,768,256]{3,2,1,0:T(8,128)S(1)} %shard_map.35.grams_ref), custom_call_target="tpu_custom_call" | custom-call | flops 201326592 | bytes 5243072 | tf_op jit(solution)/shard_map/pallas_call | solution.py:23
  33.1 0.0 collective-permute-done.5.refs_0_
  33.1 0.0 collective-permute-done.7.refs_1_
  33.1 0.6 %shard_map.32.grams_ref = f32[1,2,768,256]{3,2,1,0:T(8,128)S(1)} custom-call(bf16[12,1,2,64,1024]{4,3,2,1,0:T(8,128)(2,1)S(1)} %copy-done, bf16[4,1,2,64,256]{4,3,2,1,0:T(8,128)(2,1)S(1)} %collective-permute-done.5.refs_0_, bf16[4,1,2,64,256]{4,3,2,1,0:T(8,128)(2,1)S(1)} %collective-permute-done.7.refs_1_), custom_call_target="tpu_custom_call" | custom-call | flops 402653184 | bytes 5242880 | tf_op jit(solution)/shard_map/pallas_call | solution.py:23
  33.7 0.7 %collective-permute-done.3.far_ref = bf16[3,1,2,64,256]{4,3,2,1,0:T(8,128)(2,1)S(1)} collective-permute-done((bf16[3,1,2,64,256]{4,3,2,1,0:T(8,128)(2,1)S(1)}, bf16[3,1,2,64,256]{4,3,2,1,0:T(8,128)(2,1)S(1)}, u32[]{:S(2)}, u32[]{:S(2)}) %collective-permute-start.3) | collective-permute-done | bytes 196640 | tf_op jit(solution)/shard_map/ppermute | solution.py:18
  34.4 0.4 %shard_map.33.grams_ref = f32[1,2,768,256]{3,2,1,0:T(8,128)S(1)} custom-call(bf16[12,1,2,64,1024]{4,3,2,1,0:T(8,128)(2,1)S(1)} %copy-done, bf16[3,1,2,64,256]{4,3,2,1,0:T(8,128)(2,1)S(1)} %collective-permute-done.3.far_ref, bf16[3,1,2,64,256]{4,3,2,1,0:T(8,128)(2,1)S(1)} %collective-permute-done.2.refs_0_.near_ref, f32[1,2,768,256]{3,2,1,0:T(8,128)S(1)} %shard_map.32.grams_ref), custom_call_target="tpu_custom_call" | custom-call | flops 1610612736 | bytes 6684672 | tf_op jit(solution)/shard_map/pallas_call | solution.py:23
  34.9 0.1 collective-permute-done.1.joint_ref
  35.0 0.9 %shard_map.37 = f32[3,4,12]{2,1,0:T(4,128)S(1)} custom-call(bf16[12,1,2,64,1024]{4,3,2,1,0:T(8,128)(2,1)S(1)} %copy-done, bf16[5,1,2,64,256]{4,3,2,1,0:T(8,128)(2,1)S(1)} %collective-permute-done.1.joint_ref, f32[1,2,768,256]{3,2,1,0:T(8,128)S(1)} %shard_map.33.grams_ref, f32[4,12]{1,0:T(4,128)S(1)} %shard_map.34.own_ref, f32[4,12]{1,0:T(4,128)S(1)} %shard_map.36.second_ref), custom_call_target="tpu_custom_call" | custom-call | flops 201326592 | bytes 5047232 | tf_op jit(solution)/shard_map/pallas_call | solution.py:23
  35.9 0.0 collective-permute-start.9
  35.9 1.2 %collective-permute-done.9 = f32[3,4,12]{2,1,0:T(4,128)S(1)} collective-permute-done((f32[3,4,12]{2,1,0:T(4,128)S(1)}, f32[3,4,12]{2,1,0:T(4,128)S(1)}, u32[]{:S(2)}, u32[]{:S(2)}) %collective-permute-start.9) | collective-permute-done | bytes 608 | tf_op jit(solution)/shard_map/ppermute | solution.py:18
  37.0 0.6 %add_bitcast_fusion = f32[12,3,4]{0,2,1:T(4,128)} fusion(f32[3,4,12]{2,1,0:T(4,128)S(1)} %shard_map.37, f32[3,4,12]{2,1,0:T(4,128)S(1)} %collective-permute-done.9), kind=kLoop, calls=%fused_computation | loop fusion | flops 144 | bytes 1728 | tf_op jit(solution)/shard_map/transpose | solution.py:250
  (4 shorter events, 0.1 us)
Async XLA Ops:
  1.0 13.2 %collective-permute-start.4 = (bf16[4,1,2,64,256]{4,3,2,1,0:T(8,128)(2,1)S(1)}, bf16[4,1,2,64,256]{4,3,2,1,0:T(8,128)(2,1)S(1)}, u32[]{:S(2)}, u32[]{:S(2)}) collective-permute-start(bf16[4,1,2,64,256]{4,3,2,1,0:T(8,128)(2,1)S(1)} %slice.7.even_ref.refs_0_), channel_id=1, source_target_pairs={{0,4},{2,6},{4,8},{6,10},{8,12},{10,14},{12,16},{14,18},{16,20},{1... | collective-permute-start | bytes 786440 | tf_op jit(solution)/shard_map/ppermute | solution.py:18
  4.0 1.2 %copy-start.1 = (bf16[4,1,2,64,1024]{4,3,2,1,0:T(8,128)(2,1)S(1)}, bf16[4,1,2,64,1024]{4,3,2,1,0:T(8,128)(2,1)}, u32[]{:S(2)}) copy-start(bf16[4,1,2,64,1024]{4,3,2,1,0:T(8,128)(2,1)} %val_ref.1) | copy-start | bytes 3145732
  5.3 14.5 %collective-permute-start.6 = (bf16[4,1,2,64,256]{4,3,2,1,0:T(8,128)(2,1)S(1)}, bf16[4,1,2,64,256]{4,3,2,1,0:T(8,128)(2,1)S(1)}, u32[]{:S(2)}, u32[]{:S(2)}) collective-permute-start(bf16[4,1,2,64,256]{4,3,2,1,0:T(8,128)(2,1)S(1)} %get-tuple-element.10.even_ref.refs_1_), channel_id=1, source_target_pairs={{0,4},{2,6},{4,8},{6,10},{8,12},{10,14},{12,16},{14,18},{16,20},{1... | collective-permute-start | bytes 786440 | tf_op jit(solution)/shard_map/ppermute | solution.py:18
  6.9 21.7 %copy-start = (bf16[12,1,2,64,1024]{4,3,2,1,0:T(8,128)(2,1)S(1)}, bf16[12,1,2,64,1024]{4,3,2,1,0:T(8,128)(2,1)}, u32[]{:S(2)}) copy-start(bf16[12,1,2,64,1024]{4,3,2,1,0:T(8,128)(2,1)} %train_ref.11) | copy-start | bytes 9437188
  6.9 19.9 %collective-permute-start = (bf16[5,1,2,64,256]{4,3,2,1,0:T(8,128)(2,1)S(1)}, bf16[5,1,2,64,256]{4,3,2,1,0:T(8,128)(2,1)S(1)}, u32[]{:S(2)}, u32[]{:S(2)}) collective-permute-start(bf16[5,1,2,64,256]{4,3,2,1,0:T(8,128)(2,1)S(1)} %get-tuple-element.9.even_ref), channel_id=1, source_target_pairs={{0,4},{2,6},{4,8},{6,10},{8,12},{10,14},{12,16},{14,18},{16,20},{1... | collective-permute-start | bytes 983048 | tf_op jit(solution)/shard_map/ppermute | solution.py:18
  8.4 7.5 %collective-permute-start.2 = (bf16[3,1,2,64,256]{4,3,2,1,0:T(8,128)(2,1)S(1)}, bf16[3,1,2,64,256]{4,3,2,1,0:T(8,128)(2,1)S(1)}, u32[]{:S(2)}, u32[]{:S(2)}) collective-permute-start(bf16[3,1,2,64,256]{4,3,2,1,0:T(8,128)(2,1)S(1)} %slice.6), channel_id=1, source_target_pairs={{0,2},{2,0},{4,6},{6,4},{8,10},{10,8},{12,14},{14,12},{16,18},{18,... | collective-permute-start | bytes 589832 | tf_op jit(solution)/shard_map/ppermute | solution.py:18
  14.2 18.9 %collective-permute-start.5 = (bf16[4,1,2,64,256]{4,3,2,1,0:T(8,128)(2,1)S(1)}, bf16[4,1,2,64,256]{4,3,2,1,0:T(8,128)(2,1)S(1)}, u32[]{:S(2)}, u32[]{:S(2)}) collective-permute-start(bf16[4,1,2,64,256]{4,3,2,1,0:T(8,128)(2,1)S(1)} %shard_map.30), channel_id=1, source_target_pairs={{0,2},{2,0},{4,6},{6,4},{8,10},{10,8},{12,14},{14,12},{16,18},{18,... | collective-permute-start | bytes 786440 | tf_op jit(solution)/shard_map/ppermute | solution.py:18
  19.8 13.3 %collective-permute-start.7 = (bf16[4,1,2,64,256]{4,3,2,1,0:T(8,128)(2,1)S(1)}, bf16[4,1,2,64,256]{4,3,2,1,0:T(8,128)(2,1)S(1)}, u32[]{:S(2)}, u32[]{:S(2)}) collective-permute-start(bf16[4,1,2,64,256]{4,3,2,1,0:T(8,128)(2,1)S(1)} %shard_map.31), channel_id=1, source_target_pairs={{0,2},{2,0},{4,6},{6,4},{8,10},{10,8},{12,14},{14,12},{16,18},{18,... | collective-permute-start | bytes 786440 | tf_op jit(solution)/shard_map/ppermute | solution.py:18
  21.5 10.5 %collective-permute-start.8 = (bf16[3,1,2,64,256]{4,3,2,1,0:T(8,128)(2,1)S(1)}, bf16[3,1,2,64,256]{4,3,2,1,0:T(8,128)(2,1)S(1)}, u32[]{:S(2)}, u32[]{:S(2)}) collective-permute-start(bf16[3,1,2,64,256]{4,3,2,1,0:T(8,128)(2,1)S(1)} %slice.6), channel_id=1, source_target_pairs={{0,4},{2,6},{4,8},{6,10},{8,12},{10,14},{12,16},{14,18},{16,20},{1... | collective-permute-start | bytes 589832 | tf_op jit(solution)/shard_map/ppermute | solution.py:18
  21.5 12.9 %collective-permute-start.3 = (bf16[3,1,2,64,256]{4,3,2,1,0:T(8,128)(2,1)S(1)}, bf16[3,1,2,64,256]{4,3,2,1,0:T(8,128)(2,1)S(1)}, u32[]{:S(2)}, u32[]{:S(2)}) collective-permute-start(bf16[3,1,2,64,256]{4,3,2,1,0:T(8,128)(2,1)S(1)} %collective-permute-done.2.refs_0_.near_ref), channel_id=1, source_target_pairs={{0,4},{2,6},{4,8},{6,10},{8,12},{10,14},{12,16},{14,18},{16,20},{1... | collective-permute-start | bytes 589832 | tf_op jit(solution)/shard_map/ppermute | solution.py:18
  26.8 8.1 %collective-permute-start.1 = (bf16[5,1,2,64,256]{4,3,2,1,0:T(8,128)(2,1)S(1)}, bf16[5,1,2,64,256]{4,3,2,1,0:T(8,128)(2,1)S(1)}, u32[]{:S(2)}, u32[]{:S(2)}) collective-permute-start(bf16[5,1,2,64,256]{4,3,2,1,0:T(8,128)(2,1)S(1)} %shard_map.29), channel_id=1, source_target_pairs={{0,2},{2,0},{4,6},{6,4},{8,10},{10,8},{12,14},{14,12},{16,18},{18,... | collective-permute-start | bytes 983048 | tf_op jit(solution)/shard_map/ppermute | solution.py:18
  35.9 1.2 %collective-permute-start.9 = (f32[3,4,12]{2,1,0:T(4,128)S(1)}, f32[3,4,12]{2,1,0:T(4,128)S(1)}, u32[]{:S(2)}, u32[]{:S(2)}) collective-permute-start(f32[3,4,12]{2,1,0:T(4,128)S(1)} %shard_map.37), channel_id=1, source_target_pairs={{0,1},{1,0},{2,3},{3,2},{4,5},{5,4},{6,7},{7,6},{8,9},{9,8},{10,11... | collective-permute-start | bytes 1736 | tf_op jit(solution)/shard_map/ppermute | solution.py:18
where the time goes:
time: 37.8 us; the launch traced here: 37.6 us
  waiting for transfers between devices  15.6 us (41%)
  starting transfers between devices  14.1 us (37%)
  Pallas kernels  5.08 us (13%)
  local copies, waits for them, and re-layouts  2.22 us (6%)
  other arithmetic  0.6 us (2%)
    ppermute x10, waiting for transfers between devices, permuted(): lax.ppermute(block, axis, [(i, target(i) % size) for i in range(size)])  15.6 us
    ppermute x10, starting transfers between devices, permuted(): lax.ppermute(block, axis, [(i, target(i) % size) for i in range(size)])  14.1 us
    pallas_call x10, Pallas kernels, call(): pl.pallas_call(kernel, out_shape=out_shape, in_specs=specs, out_specs=jax...  5.08 us
    unnamed x4, local copies, waits for them, and re-layouts  1.23 us
    slice x1, local copies, waits for them, and re-layouts, local(): parts = [val[..., :depth]] + parts  0.97 us
  transfers between devices with their start and end apart: 10, of which 7 were waited for; matrix products, arithmetic and copies ran while one was open for 0% of the time, Pallas kernels for 11%

commit v1 on v0

--- a/solution.py
+++ b/solution.py
@@ -8,7 +8,7 @@
 from jax.sharding import PartitionSpec as P
 
 CUTS = 4
-GROUP = 4
+GROUP = 12
 
 VMEM = pl.BlockSpec(memory_space=pltpu.VMEM)
 

time: 37.8 us -> 37.8 us (level)
  no operation moved by 1% of the time
where the time goes in v1:
time: 37.8 us; the launch traced here: 37.6 us
  waiting for transfers between devices  15.6 us (41%)
  starting transfers between devices  14.1 us (37%)
  Pallas kernels  5.06 us (13%)
  local copies, waits for them, and re-layouts  2.22 us (6%)
  other arithmetic  0.6 us (2%)
    ppermute x10, waiting for transfers between devices, permuted(): lax.ppermute(block, axis, [(i, target(i) % size) for i in range(size)])  15.6 us
    ppermute x10, starting transfers between devices, permuted(): lax.ppermute(block, axis, [(i, target(i) % size) for i in range(size)])  14.1 us
    pallas_call x10, Pallas kernels, call(): pl.pallas_call(kernel, out_shape=out_shape, in_specs=specs, out_specs=jax...  5.06 us
    unnamed x4, local copies, waits for them, and re-layouts  1.23 us
    slice x1, local copies, waits for them, and re-layouts, local(): parts = [val[..., :depth]] + parts  0.97 us
  transfers between devices with their start and end apart: 10, of which 7 were waited for; matrix products, arithmetic and copies ran while one was open for 0% of the time, Pallas kernels for 11%

profile of v1, /device:TPU:0, one launch (start us, length us, event | category | flops | bytes accessed | tf_op | source)
XLA Modules:
  0.0 37.6 jit_solution(4337724253063936974)
XLA Ops:
  0.0 1.0 %slice.7.even_ref.refs_0_ = bf16[4,1,2,64,256]{4,3,2,1,0:T(8,128)(2,1)S(1)} slice(bf16[4,1,2,64,1024]{4,3,2,1,0:T(8,128)(2,1)} %val_ref.1), slice={[0:4], [0:1], [0:2], [0:64], [0:256]} | slice | bytes 524288 | tf_op jit(solution)/shard_map/slice | solution.py:227
  1.0 3.0 %collective-permute-start.4 = (bf16[4,1,2,64,256]{4,3,2,1,0:T(8,128)(2,1)S(1)}, bf16[4,1,2,64,256]{4,3,2,1,0:T(8,128)(2,1)S(1)}, u32[]{:S(2)}, u32[]{:S(2)}) collective-permute-start(bf16[4,1,2,64,256]{4,3,2,1,0:T(8,128)(2,1)S(1)} %slice.7.even_ref.refs_0_), channel_id=1, source_target_pairs={{0,4},{2,6},{4,8},{6,10},{8,12},{10,14},{12,16},{14,18},{16,20},{1... | collective-permute-start | bytes 786440 | tf_op jit(solution)/shard_map/ppermute | solution.py:18
  4.0 0.0 copy-start.1
  4.0 1.2 %copy-done.1 = bf16[4,1,2,64,1024]{4,3,2,1,0:T(8,128)(2,1)S(1)} copy-done((bf16[4,1,2,64,1024]{4,3,2,1,0:T(8,128)(2,1)S(1)}, bf16[4,1,2,64,1024]{4,3,2,1,0:T(8,128)(2,1)}, u32[]{:S(2)}) %copy-start.1) | copy-done | bytes 1048600
  5.2 0.1 shard_map.28
  5.3 1.6 %collective-permute-start.6 = (bf16[4,1,2,64,256]{4,3,2,1,0:T(8,128)(2,1)S(1)}, bf16[4,1,2,64,256]{4,3,2,1,0:T(8,128)(2,1)S(1)}, u32[]{:S(2)}, u32[]{:S(2)}) collective-permute-start(bf16[4,1,2,64,256]{4,3,2,1,0:T(8,128)(2,1)S(1)} %get-tuple-element.10.even_ref.refs_1_), channel_id=1, source_target_pairs={{0,4},{2,6},{4,8},{6,10},{8,12},{10,14},{12,16},{14,18},{16,20},{1... | collective-permute-start | bytes 786440 | tf_op jit(solution)/shard_map/ppermute | solution.py:18
  6.9 0.0 copy-start
  6.9 1.5 %collective-permute-start = (bf16[5,1,2,64,256]{4,3,2,1,0:T(8,128)(2,1)S(1)}, bf16[5,1,2,64,256]{4,3,2,1,0:T(8,128)(2,1)S(1)}, u32[]{:S(2)}, u32[]{:S(2)}) collective-permute-start(bf16[5,1,2,64,256]{4,3,2,1,0:T(8,128)(2,1)S(1)} %get-tuple-element.9.even_ref), channel_id=1, source_target_pairs={{0,4},{2,6},{4,8},{6,10},{8,12},{10,14},{12,16},{14,18},{16,20},{1... | collective-permute-start | bytes 983048 | tf_op jit(solution)/shard_map/ppermute | solution.py:18
  8.4 1.6 %collective-permute-start.2 = (bf16[3,1,2,64,256]{4,3,2,1,0:T(8,128)(2,1)S(1)}, bf16[3,1,2,64,256]{4,3,2,1,0:T(8,128)(2,1)S(1)}, u32[]{:S(2)}, u32[]{:S(2)}) collective-permute-start(bf16[3,1,2,64,256]{4,3,2,1,0:T(8,128)(2,1)S(1)} %slice.6), channel_id=1, source_target_pairs={{0,2},{2,0},{4,6},{6,4},{8,10},{10,8},{12,14},{14,12},{16,18},{18,... | collective-permute-start | bytes 589832 | tf_op jit(solution)/shard_map/ppermute | solution.py:18
  10.0 4.2 %collective-permute-done.4.odd_ref.refs_0_ = bf16[4,1,2,64,256]{4,3,2,1,0:T(8,128)(2,1)S(1)} collective-permute-done((bf16[4,1,2,64,256]{4,3,2,1,0:T(8,128)(2,1)S(1)}, bf16[4,1,2,64,256]{4,3,2,1,0:T(8,128)(2,1)S(1)}, u32[]{:S(2)}, u32[]{:S(2)}) %collective-permute-start.4) | collective-permute-done | bytes 262176 | tf_op jit(solution)/shard_map/ppermute | solution.py:18
  14.2 1.7 %collective-permute-start.5 = (bf16[4,1,2,64,256]{4,3,2,1,0:T(8,128)(2,1)S(1)}, bf16[4,1,2,64,256]{4,3,2,1,0:T(8,128)(2,1)S(1)}, u32[]{:S(2)}, u32[]{:S(2)}) collective-permute-start(bf16[4,1,2,64,256]{4,3,2,1,0:T(8,128)(2,1)S(1)} %shard_map.30), channel_id=1, source_target_pairs={{0,2},{2,0},{4,6},{6,4},{8,10},{10,8},{12,14},{14,12},{16,18},{18,... | collective-permute-start | bytes 786440 | tf_op jit(solution)/shard_map/ppermute | solution.py:18
  15.9 0.0 collective-permute-done.2.refs_0_.near_ref
  15.9 3.9 %collective-permute-done.6.odd_ref.refs_1_ = bf16[4,1,2,64,256]{4,3,2,1,0:T(8,128)(2,1)S(1)} collective-permute-done((bf16[4,1,2,64,256]{4,3,2,1,0:T(8,128)(2,1)S(1)}, bf16[4,1,2,64,256]{4,3,2,1,0:T(8,128)(2,1)S(1)}, u32[]{:S(2)}, u32[]{:S(2)}) %collective-permute-start.6) | collective-permute-done | bytes 262176 | tf_op jit(solution)/shard_map/ppermute | solution.py:18
  19.8 1.7 %collective-permute-start.7 = (bf16[4,1,2,64,256]{4,3,2,1,0:T(8,128)(2,1)S(1)}, bf16[4,1,2,64,256]{4,3,2,1,0:T(8,128)(2,1)S(1)}, u32[]{:S(2)}, u32[]{:S(2)}) collective-permute-start(bf16[4,1,2,64,256]{4,3,2,1,0:T(8,128)(2,1)S(1)} %shard_map.31), channel_id=1, source_target_pairs={{0,2},{2,0},{4,6},{6,4},{8,10},{10,8},{12,14},{14,12},{16,18},{18,... | collective-permute-start | bytes 786440 | tf_op jit(solution)/shard_map/ppermute | solution.py:18
  21.5 0.0 collective-permute-start.8
  21.5 1.3 %collective-permute-start.3 = (bf16[3,1,2,64,256]{4,3,2,1,0:T(8,128)(2,1)S(1)}, bf16[3,1,2,64,256]{4,3,2,1,0:T(8,128)(2,1)S(1)}, u32[]{:S(2)}, u32[]{:S(2)}) collective-permute-start(bf16[3,1,2,64,256]{4,3,2,1,0:T(8,128)(2,1)S(1)} %collective-permute-done.2.refs_0_.near_ref), channel_id=1, source_target_pairs={{0,4},{2,6},{4,8},{6,10},{8,12},{10,14},{12,16},{14,18},{16,20},{1... | collective-permute-start | bytes 589832 | tf_op jit(solution)/shard_map/ppermute | solution.py:18
  22.8 4.0 %collective-permute-done.odd_ref.refs_2_.joint_ref = bf16[5,1,2,64,256]{4,3,2,1,0:T(8,128)(2,1)S(1)} collective-permute-done((bf16[5,1,2,64,256]{4,3,2,1,0:T(8,128)(2,1)S(1)}, bf16[5,1,2,64,256]{4,3,2,1,0:T(8,128)(2,1)S(1)}, u32[]{:S(2)}, u32[]{:S(2)}) %collective-permute-start) | collective-permute-done | bytes 327712 | tf_op jit(solution)/shard_map/ppermute | solution.py:18
  26.8 1.7 %collective-permute-start.1 = (bf16[5,1,2,64,256]{4,3,2,1,0:T(8,128)(2,1)S(1)}, bf16[5,1,2,64,256]{4,3,2,1,0:T(8,128)(2,1)S(1)}, u32[]{:S(2)}, u32[]{:S(2)}) collective-permute-start(bf16[5,1,2,64,256]{4,3,2,1,0:T(8,128)(2,1)S(1)} %shard_map.29), channel_id=1, source_target_pairs={{0,2},{2,0},{4,6},{6,4},{8,10},{10,8},{12,14},{14,12},{16,18},{18,... | collective-permute-start | bytes 983048 | tf_op jit(solution)/shard_map/ppermute | solution.py:18
  28.6 0.0 copy-done
  28.6 1.1 %shard_map.34.own_ref = f32[4,12]{1,0:T(4,128)S(1)} custom-call(bf16[12,1,2,64,1024]{4,3,2,1,0:T(8,128)(2,1)S(1)} %copy-done, bf16[4,1,2,64,256]{4,3,2,1,0:T(8,128)(2,1)S(1)} %slice.7.even_ref.refs_0_, bf16[4,1,2,64,256]{4,3,2,1,0:T(8,128)(2,1)S(1)} %get-tuple-element.10.even_ref.refs_1_, bf16[4,1,2,64,256]{4,3,2,1,0:T(8,128)(2,1)S(1)} %get-tuple-element.11.refs_2_, ...), custom_call_target="tpu_custom_call" | custom-call | flops 805306368 | bytes 4194496 | tf_op jit(solution)/shard_map/pallas_call | solution.py:23
  29.7 0.8 %shard_map.35.grams_ref = f32[1,2,768,256]{3,2,1,0:T(8,128)S(1)} custom-call(bf16[12,1,2,64,1024]{4,3,2,1,0:T(8,128)(2,1)S(1)} %copy-done, bf16[4,1,2,64,256]{4,3,2,1,0:T(8,128)(2,1)S(1)} %collective-permute-done.4.odd_ref.refs_0_, bf16[4,1,2,64,256]{4,3,2,1,0:T(8,128)(2,1)S(1)} %collective-permute-done.6.odd_ref.refs_1_, ...), custom_call_target="tpu_custom_call" | custom-call | flops 805306368 | bytes 5570560 | tf_op jit(solution)/shard_map/pallas_call | solution.py:23
  30.5 1.6 %collective-permute-done.8.detour_ref = bf16[3,1,2,64,256]{4,3,2,1,0:T(8,128)(2,1)S(1)} collective-permute-done((bf16[3,1,2,64,256]{4,3,2,1,0:T(8,128)(2,1)S(1)}, bf16[3,1,2,64,256]{4,3,2,1,0:T(8,128)(2,1)S(1)}, u32[]{:S(2)}, u32[]{:S(2)}) %collective-permute-start.8) | collective-permute-done | bytes 196640 | tf_op jit(solution)/shard_map/ppermute | solution.py:18
  32.1 1.0 %shard_map.36.second_ref = f32[4,12]{1,0:T(4,128)S(1)} custom-call(bf16[12,1,2,64,1024]{4,3,2,1,0:T(8,128)(2,1)S(1)} %copy-done, bf16[3,1,2,64,256]{4,3,2,1,0:T(8,128)(2,1)S(1)} %collective-permute-done.8.detour_ref, bf16[5,1,2,64,256]{4,3,2,1,0:T(8,128)(2,1)S(1)} %collective-permute-done.odd_ref.refs_2_.joint_ref, f32[1,2,768,256]{3,2,1,0:T(8,128)S(1)} %shard_map.35.grams_ref), custom_call_target="tpu_custom_call" | custom-call | flops 201326592 | bytes 5243072 | tf_op jit(solution)/shard_map/pallas_call | solution.py:23
  33.1 0.0 collective-permute-done.5.refs_0_
  33.1 0.0 collective-permute-done.7.refs_1_
  33.1 0.6 %shard_map.32.grams_ref = f32[1,2,768,256]{3,2,1,0:T(8,128)S(1)} custom-call(bf16[12,1,2,64,1024]{4,3,2,1,0:T(8,128)(2,1)S(1)} %copy-done, bf16[4,1,2,64,256]{4,3,2,1,0:T(8,128)(2,1)S(1)} %collective-permute-done.5.refs_0_, bf16[4,1,2,64,256]{4,3,2,1,0:T(8,128)(2,1)S(1)} %collective-permute-done.7.refs_1_), custom_call_target="tpu_custom_call" | custom-call | flops 402653184 | bytes 5242880 | tf_op jit(solution)/shard_map/pallas_call | solution.py:23
  33.7 0.7 %collective-permute-done.3.far_ref = bf16[3,1,2,64,256]{4,3,2,1,0:T(8,128)(2,1)S(1)} collective-permute-done((bf16[3,1,2,64,256]{4,3,2,1,0:T(8,128)(2,1)S(1)}, bf16[3,1,2,64,256]{4,3,2,1,0:T(8,128)(2,1)S(1)}, u32[]{:S(2)}, u32[]{:S(2)}) %collective-permute-start.3) | collective-permute-done | bytes 196640 | tf_op jit(solution)/shard_map/ppermute | solution.py:18
  34.4 0.4 %shard_map.33.grams_ref = f32[1,2,768,256]{3,2,1,0:T(8,128)S(1)} custom-call(bf16[12,1,2,64,1024]{4,3,2,1,0:T(8,128)(2,1)S(1)} %copy-done, bf16[3,1,2,64,256]{4,3,2,1,0:T(8,128)(2,1)S(1)} %collective-permute-done.3.far_ref, bf16[3,1,2,64,256]{4,3,2,1,0:T(8,128)(2,1)S(1)} %collective-permute-done.2.refs_0_.near_ref, f32[1,2,768,256]{3,2,1,0:T(8,128)S(1)} %shard_map.32.grams_ref), custom_call_target="tpu_custom_call" | custom-call | flops 1610612736 | bytes 6684672 | tf_op jit(solution)/shard_map/pallas_call | solution.py:23
  34.8 0.1 collective-permute-done.1.joint_ref
  35.0 0.9 %shard_map.37 = f32[3,4,12]{2,1,0:T(4,128)S(1)} custom-call(bf16[12,1,2,64,1024]{4,3,2,1,0:T(8,128)(2,1)S(1)} %copy-done, bf16[5,1,2,64,256]{4,3,2,1,0:T(8,128)(2,1)S(1)} %collective-permute-done.1.joint_ref, f32[1,2,768,256]{3,2,1,0:T(8,128)S(1)} %shard_map.33.grams_ref, f32[4,12]{1,0:T(4,128)S(1)} %shard_map.34.own_ref, f32[4,12]{1,0:T(4,128)S(1)} %shard_map.36.second_ref), custom_call_target="tpu_custom_call" | custom-call | flops 201326592 | bytes 5047232 | tf_op jit(solution)/shard_map/pallas_call | solution.py:23
  35.9 0.0 collective-permute-start.9
  35.9 1.2 %collective-permute-done.9 = f32[3,4,12]{2,1,0:T(4,128)S(1)} collective-permute-done((f32[3,4,12]{2,1,0:T(4,128)S(1)}, f32[3,4,12]{2,1,0:T(4,128)S(1)}, u32[]{:S(2)}, u32[]{:S(2)}) %collective-permute-start.9) | collective-permute-done | bytes 608 | tf_op jit(solution)/shard_map/ppermute | solution.py:18
  37.1 0.6 %add_bitcast_fusion = f32[12,3,4]{0,2,1:T(4,128)} fusion(f32[3,4,12]{2,1,0:T(4,128)S(1)} %shard_map.37, f32[3,4,12]{2,1,0:T(4,128)S(1)} %collective-permute-done.9), kind=kLoop, calls=%fused_computation | loop fusion | flops 144 | bytes 1728 | tf_op jit(solution)/shard_map/transpose | solution.py:250
  (4 shorter events, 0.1 us)
Async XLA Ops:
  1.0 13.2 %collective-permute-start.4 = (bf16[4,1,2,64,256]{4,3,2,1,0:T(8,128)(2,1)S(1)}, bf16[4,1,2,64,256]{4,3,2,1,0:T(8,128)(2,1)S(1)}, u32[]{:S(2)}, u32[]{:S(2)}) collective-permute-start(bf16[4,1,2,64,256]{4,3,2,1,0:T(8,128)(2,1)S(1)} %slice.7.even_ref.refs_0_), channel_id=1, source_target_pairs={{0,4},{2,6},{4,8},{6,10},{8,12},{10,14},{12,16},{14,18},{16,20},{1... | collective-permute-start | bytes 786440 | tf_op jit(solution)/shard_map/ppermute | solution.py:18
  4.0 1.2 %copy-start.1 = (bf16[4,1,2,64,1024]{4,3,2,1,0:T(8,128)(2,1)S(1)}, bf16[4,1,2,64,1024]{4,3,2,1,0:T(8,128)(2,1)}, u32[]{:S(2)}) copy-start(bf16[4,1,2,64,1024]{4,3,2,1,0:T(8,128)(2,1)} %val_ref.1) | copy-start | bytes 3145732
  5.3 14.5 %collective-permute-start.6 = (bf16[4,1,2,64,256]{4,3,2,1,0:T(8,128)(2,1)S(1)}, bf16[4,1,2,64,256]{4,3,2,1,0:T(8,128)(2,1)S(1)}, u32[]{:S(2)}, u32[]{:S(2)}) collective-permute-start(bf16[4,1,2,64,256]{4,3,2,1,0:T(8,128)(2,1)S(1)} %get-tuple-element.10.even_ref.refs_1_), channel_id=1, source_target_pairs={{0,4},{2,6},{4,8},{6,10},{8,12},{10,14},{12,16},{14,18},{16,20},{1... | collective-permute-start | bytes 786440 | tf_op jit(solution)/shard_map/ppermute | solution.py:18
  6.9 21.7 %copy-start = (bf16[12,1,2,64,1024]{4,3,2,1,0:T(8,128)(2,1)S(1)}, bf16[12,1,2,64,1024]{4,3,2,1,0:T(8,128)(2,1)}, u32[]{:S(2)}) copy-start(bf16[12,1,2,64,1024]{4,3,2,1,0:T(8,128)(2,1)} %train_ref.11) | copy-start | bytes 9437188
  6.9 19.9 %collective-permute-start = (bf16[5,1,2,64,256]{4,3,2,1,0:T(8,128)(2,1)S(1)}, bf16[5,1,2,64,256]{4,3,2,1,0:T(8,128)(2,1)S(1)}, u32[]{:S(2)}, u32[]{:S(2)}) collective-permute-start(bf16[5,1,2,64,256]{4,3,2,1,0:T(8,128)(2,1)S(1)} %get-tuple-element.9.even_ref), channel_id=1, source_target_pairs={{0,4},{2,6},{4,8},{6,10},{8,12},{10,14},{12,16},{14,18},{16,20},{1... | collective-permute-start | bytes 983048 | tf_op jit(solution)/shard_map/ppermute | solution.py:18
  8.4 7.5 %collective-permute-start.2 = (bf16[3,1,2,64,256]{4,3,2,1,0:T(8,128)(2,1)S(1)}, bf16[3,1,2,64,256]{4,3,2,1,0:T(8,128)(2,1)S(1)}, u32[]{:S(2)}, u32[]{:S(2)}) collective-permute-start(bf16[3,1,2,64,256]{4,3,2,1,0:T(8,128)(2,1)S(1)} %slice.6), channel_id=1, source_target_pairs={{0,2},{2,0},{4,6},{6,4},{8,10},{10,8},{12,14},{14,12},{16,18},{18,... | collective-permute-start | bytes 589832 | tf_op jit(solution)/shard_map/ppermute | solution.py:18
  14.2 18.9 %collective-permute-start.5 = (bf16[4,1,2,64,256]{4,3,2,1,0:T(8,128)(2,1)S(1)}, bf16[4,1,2,64,256]{4,3,2,1,0:T(8,128)(2,1)S(1)}, u32[]{:S(2)}, u32[]{:S(2)}) collective-permute-start(bf16[4,1,2,64,256]{4,3,2,1,0:T(8,128)(2,1)S(1)} %shard_map.30), channel_id=1, source_target_pairs={{0,2},{2,0},{4,6},{6,4},{8,10},{10,8},{12,14},{14,12},{16,18},{18,... | collective-permute-start | bytes 786440 | tf_op jit(solution)/shard_map/ppermute | solution.py:18
  19.8 13.3 %collective-permute-start.7 = (bf16[4,1,2,64,256]{4,3,2,1,0:T(8,128)(2,1)S(1)}, bf16[4,1,2,64,256]{4,3,2,1,0:T(8,128)(2,1)S(1)}, u32[]{:S(2)}, u32[]{:S(2)}) collective-permute-start(bf16[4,1,2,64,256]{4,3,2,1,0:T(8,128)(2,1)S(1)} %shard_map.31), channel_id=1, source_target_pairs={{0,2},{2,0},{4,6},{6,4},{8,10},{10,8},{12,14},{14,12},{16,18},{18,... | collective-permute-start | bytes 786440 | tf_op jit(solution)/shard_map/ppermute | solution.py:18
  21.5 10.5 %collective-permute-start.8 = (bf16[3,1,2,64,256]{4,3,2,1,0:T(8,128)(2,1)S(1)}, bf16[3,1,2,64,256]{4,3,2,1,0:T(8,128)(2,1)S(1)}, u32[]{:S(2)}, u32[]{:S(2)}) collective-permute-start(bf16[3,1,2,64,256]{4,3,2,1,0:T(8,128)(2,1)S(1)} %slice.6), channel_id=1, source_target_pairs={{0,4},{2,6},{4,8},{6,10},{8,12},{10,14},{12,16},{14,18},{16,20},{1... | collective-permute-start | bytes 589832 | tf_op jit(solution)/shard_map/ppermute | solution.py:18
  21.5 12.9 %collective-permute-start.3 = (bf16[3,1,2,64,256]{4,3,2,1,0:T(8,128)(2,1)S(1)}, bf16[3,1,2,64,256]{4,3,2,1,0:T(8,128)(2,1)S(1)}, u32[]{:S(2)}, u32[]{:S(2)}) collective-permute-start(bf16[3,1,2,64,256]{4,3,2,1,0:T(8,128)(2,1)S(1)} %collective-permute-done.2.refs_0_.near_ref), channel_id=1, source_target_pairs={{0,4},{2,6},{4,8},{6,10},{8,12},{10,14},{12,16},{14,18},{16,20},{1... | collective-permute-start | bytes 589832 | tf_op jit(solution)/shard_map/ppermute | solution.py:18
  26.8 8.1 %collective-permute-start.1 = (bf16[5,1,2,64,256]{4,3,2,1,0:T(8,128)(2,1)S(1)}, bf16[5,1,2,64,256]{4,3,2,1,0:T(8,128)(2,1)S(1)}, u32[]{:S(2)}, u32[]{:S(2)}) collective-permute-start(bf16[5,1,2,64,256]{4,3,2,1,0:T(8,128)(2,1)S(1)} %shard_map.29), channel_id=1, source_target_pairs={{0,2},{2,0},{4,6},{6,4},{8,10},{10,8},{12,14},{14,12},{16,18},{18,... | collective-permute-start | bytes 983048 | tf_op jit(solution)/shard_map/ppermute | solution.py:18
  35.9 1.2 %collective-permute-start.9 = (f32[3,4,12]{2,1,0:T(4,128)S(1)}, f32[3,4,12]{2,1,0:T(4,128)S(1)}, u32[]{:S(2)}, u32[]{:S(2)}) collective-permute-start(f32[3,4,12]{2,1,0:T(4,128)S(1)} %shard_map.37), channel_id=1, source_target_pairs={{0,1},{1,0},{2,3},{3,2},{4,5},{5,4},{6,7},{7,6},{8,9},{9,8},{10,11... | collective-permute-start | bytes 1736 | tf_op jit(solution)/shard_map/ppermute | solution.py:18
